TPU v7x, 256 devices: a whole 4x4x8 slice. The times are simulated.
256 devices in a mesh: dp: 32 (over z_lo, x, core), blk: 8 (over y, z_hi).
Axes of the slice: x: 4, y: 4, z: 8 (z_hi: 2, z_lo: 4; z = z_hi * 4 + z_lo), core: 2. Of those that a mesh axis runs over, the one named last changes fastest.
Arguments:
- tokens: bfloat16 [4096, 8192], P('dp', 'blk'), may hold values from -6 to 6
- gate_right: bfloat16 [256, 32, 448], P(None, 'blk'), may hold values from -0.375 to 0.375
- gate_left: bfloat16 [448, 32, 448], P(None, 'blk'), may hold values from -0.25 to 0.25
- upward_right: bfloat16 [256, 32, 448], P(None, 'blk'), may hold values from -0.375 to 0.375
- upward_left: bfloat16 [448, 32, 448], P(None, 'blk'), may hold values from -0.25 to 0.25
- down_right: bfloat16 [448, 32, 256], P(None, 'blk'), may hold values from -0.25 to 0.25
- down_left: bfloat16 [256, 32, 256], P(None, 'blk'), may hold values from -0.375 to 0.375
- cotangent: bfloat16 [4096, 8192], P('dp', 'blk'), may hold values from -6 to 6
Outputs:
- mixed: bfloat16 [4096, 8192], P('dp', 'blk')
- grad_tokens: bfloat16 [4096, 8192], P('dp', 'blk')
- gate_right_grad: float32 [256, 32, 448], P('dp', 'blk')
- gate_left_grad: float32 [448, 32, 448], P('dp', 'blk')
- upward_right_grad: float32 [256, 32, 448], P('dp', 'blk')
- upward_left_grad: float32 [448, 32, 448], P('dp', 'blk')
- down_right_grad: float32 [448, 32, 256], P('dp', 'blk')
- down_left_grad: float32 [256, 32, 256], P('dp', 'blk')
All inputs are finite; a program needn't handle non-finite values.
Results may differ from a plain program's by a relative error of at most 0.0072.
Values may be sent and summed in bfloat16 or wider, within the bound.
A program may use at most 128 MiB of HBM per device.

v0:
```python
import jax
import jax.numpy as jnp
from jax import lax
from jax.sharding import PartitionSpec as P

NB = 32


def right_apply(source, weight_four):
    return jnp.einsum(
        "tkb,bkjr->jkrt", source, weight_four, preferred_element_type=jnp.float32
    ).astype(jnp.bfloat16)


def left_apply(exchanged, weight_left):
    merged = exchanged.reshape(
        exchanged.shape[0], exchanged.shape[1] * exchanged.shape[2], exchanged.shape[3]
    )
    result = jnp.einsum("jmt,mjn->jnt", merged, weight_left, preferred_element_type=jnp.float32)
    return (result, merged)


def back_left(gradient, weight_left, blocks_all):
    flowed = jnp.einsum(
        "jnt,mjn->jmt", gradient, weight_left, preferred_element_type=jnp.float32
    ).astype(jnp.bfloat16)
    return flowed.reshape(
        flowed.shape[0], blocks_all, flowed.shape[1] // blocks_all, flowed.shape[2]
    )


def term_left(seen, gradient, grad_scale):
    return grad_scale * jnp.einsum(
        "jmt,jnt->mjn", seen, gradient, preferred_element_type=jnp.float32
    )


def term_down_left(seen, upstream, grad_scale):
    return grad_scale * jnp.einsum(
        "jmt,tjn->mjn", seen, upstream, preferred_element_type=jnp.float32
    )


def term_down_right(hidden, down_back, grad_scale, row_count):
    result = jnp.einsum("knt,jkst->nkjs", hidden, down_back, preferred_element_type=jnp.float32)
    return grad_scale * result.reshape(
        row_count, result.shape[1], result.shape[2] * result.shape[3]
    )


def term_right(inputs, back_values, grad_scale, row_count):
    result = jnp.einsum("tkb,jkrt->bkjr", inputs, back_values, preferred_element_type=jnp.float32)
    return grad_scale * result.reshape(
        row_count, result.shape[1], result.shape[2] * result.shape[3]
    )


def local(
    tokens, gate_right, gate_left, upward_right, upward_left, down_right, down_left, cotangent
):
    token_rows = tokens.shape[0]
    local_blocks = gate_right.shape[1]
    width_block = gate_right.shape[0]
    hidden_block = gate_left.shape[0]
    data_size = lax.axis_size("dp")
    grad_scale = float(token_rows * data_size) ** (-0.5)
    inputs = tokens.reshape(token_rows, local_blocks, width_block)
    gate_four = gate_right.reshape(width_block, local_blocks, NB, hidden_block // NB)
    upward_four = upward_right.reshape(width_block, local_blocks, NB, hidden_block // NB)
    down_four = down_right.reshape(hidden_block, local_blocks, NB, width_block // NB)
    gate_mixed = right_apply(inputs, gate_four)
    upward_mixed = right_apply(inputs, upward_four)
    gate_pre, gate_seen = left_apply(
        lax.all_to_all(gate_mixed, "blk", split_axis=0, concat_axis=1, tiled=True),
        weight_left=gate_left,
    )
    upward_pre, upward_seen = left_apply(
        lax.all_to_all(upward_mixed, "blk", split_axis=0, concat_axis=1, tiled=True),
        weight_left=upward_left,
    )
    gate_sigmoid = jax.nn.sigmoid(gate_pre)
    activated = gate_pre * gate_sigmoid
    hidden = (activated * upward_pre).astype(jnp.bfloat16)
    down_mixed = jnp.einsum(
        "knt,nkjs->jkst", hidden, down_four, preferred_element_type=jnp.float32
    ).astype(jnp.bfloat16)
    down_out, down_seen = left_apply(
        lax.all_to_all(down_mixed, "blk", split_axis=0, concat_axis=1, tiled=True),
        weight_left=down_left,
    )
    mixed = (
        jnp.transpose(down_out, (2, 0, 1))
        .reshape(token_rows, local_blocks * width_block)
        .astype(jnp.bfloat16)
    )
    upstream = cotangent.reshape(token_rows, local_blocks, width_block)
    down_flow = jnp.einsum(
        "tjn,mjn->jmt", upstream, down_left, preferred_element_type=jnp.float32
    ).astype(jnp.bfloat16)
    down_flow = down_flow.reshape(local_blocks, NB, width_block // NB, token_rows)
    down_back = lax.all_to_all(down_flow, "blk", split_axis=1, concat_axis=0, tiled=True)
    hidden_flow = jnp.einsum(
        "jkst,nkjs->knt", down_back, down_four, preferred_element_type=jnp.float32
    )
    gate_grad = (
        hidden_flow * upward_pre * gate_sigmoid * (1.0 + gate_pre * (1.0 - gate_sigmoid))
    ).astype(jnp.bfloat16)
    upward_grad = (hidden_flow * activated).astype(jnp.bfloat16)
    gate_flow = back_left(gate_grad, gate_left, NB)
    upward_flow = back_left(upward_grad, upward_left, NB)
    gate_back = lax.all_to_all(gate_flow, "blk", split_axis=1, concat_axis=0, tiled=True)
    upward_back = lax.all_to_all(upward_flow, "blk", split_axis=1, concat_axis=0, tiled=True)
    token_flow = jnp.einsum(
        "jkrt,bkjr->tkb", gate_back, gate_four, preferred_element_type=jnp.float32
    )
    token_flow = token_flow + jnp.einsum(
        "jkrt,bkjr->tkb", upward_back, upward_four, preferred_element_type=jnp.float32
    )
    grad_tokens = token_flow.reshape(token_rows, local_blocks * width_block).astype(jnp.bfloat16)
    whole_terms = (
        term_right(inputs, gate_back, grad_scale, width_block),
        term_left(gate_seen, gate_grad, grad_scale),
        term_right(inputs, upward_back, grad_scale, width_block),
        term_left(upward_seen, upward_grad, grad_scale),
        term_down_right(hidden, down_back, grad_scale, hidden_block),
        term_down_left(down_seen, upstream, grad_scale),
    )
    (
        gate_right_grad,
        gate_left_grad,
        upward_right_grad,
        upward_left_grad,
        down_right_grad,
        down_left_grad,
    ) = (
        lax.psum_scatter(whole_terms[0], "dp", scatter_dimension=0, tiled=True),
        lax.psum_scatter(whole_terms[1], "dp", scatter_dimension=0, tiled=True),
        lax.psum_scatter(whole_terms[2], "dp", scatter_dimension=0, tiled=True),
        lax.psum_scatter(whole_terms[3], "dp", scatter_dimension=0, tiled=True),
        lax.psum_scatter(whole_terms[4], "dp", scatter_dimension=0, tiled=True),
        lax.psum_scatter(whole_terms[5], "dp", scatter_dimension=0, tiled=True),
    )
    return (
        mixed,
        grad_tokens,
        gate_right_grad,
        gate_left_grad,
        upward_right_grad,
        upward_left_grad,
        down_right_grad,
        down_left_grad,
    )


def solution(mesh):
    placed = (
        P("dp", "blk"),
        P(None, "blk", None),
        P(None, "blk", None),
        P(None, "blk", None),
        P(None, "blk", None),
        P(None, "blk", None),
        P(None, "blk", None),
        P("dp", "blk"),
    )
    return jax.shard_map(
        local,
        mesh=mesh,
        in_specs=placed,
        out_specs=(
            P("dp", "blk"),
            P("dp", "blk"),
            P("dp", "blk", None),
            P("dp", "blk", None),
            P("dp", "blk", None),
            P("dp", "blk", None),
            P("dp", "blk", None),
            P("dp", "blk", None),
        ),
        check_vma=False,
    )
```

profile of v0, /device:TPU:1, one launch (start us, length us, event | category | flops | bytes accessed | tf_op | source)
XLA Modules:
  0.0 575.1 jit_solution(7304396960128916856)
XLA Ops:
  9.4 11.6 %all-to-all-start.3 = ((bf16[4,32,8,128]{3,2,0,1:T(8,128)(2,1)}), bf16[4,32,8,128]{3,2,0,1:T(8,128)(2,1)S(1)}, u32[]{:S(2)}, u32[]{:S(2)}) async-start(bf16[4,32,8,128]{3,2,0,1:T(8,128)(2,1)} %copy.217), calls=%async_computation.3 | async-start | bytes 524288 | tf_op jit(solution)/shard_map/all_to_all | solution.py:101
  24.5 6.8 %all-to-all-done.3 = bf16[4,32,8,128]{3,2,0,1:T(8,128)(2,1)S(1)} async-done(((bf16[4,32,8,128]{3,2,0,1:T(8,128)(2,1)}), bf16[4,32,8,128]{3,2,0,1:T(8,128)(2,1)S(1)}, u32[]{:S(2)}, u32[]{:S(2)}) %all-to-all-start.3) | async-done | bytes 262176 | tf_op jit(solution)/shard_map/all_to_all | solution.py:101
  31.3 3.5 all-to-all-start
  38.0 7.8 %all-to-all-done = bf16[32,4,14,128]{3,1,2,0:T(4,128)(2,1)S(1)} async-done(((bf16[32,4,14,128]{3,1,2,0:T(4,128)(2,1)}), bf16[32,4,14,128]{3,1,2,0:T(4,128)(2,1)S(1)}, u32[]{:S(2)}, u32[]{:S(2)}) %all-to-all-start) | async-done | bytes 458784 | tf_op jit(solution)/shard_map/all_to_all | solution.py:74
  45.8 3.5 all-to-all-start.1
  52.7 7.8 %all-to-all-done.1 = bf16[32,4,14,128]{3,1,2,0:T(4,128)(2,1)S(1)} async-done(((bf16[32,4,14,128]{3,1,2,0:T(4,128)(2,1)}), bf16[32,4,14,128]{3,1,2,0:T(4,128)(2,1)S(1)}, u32[]{:S(2)}, u32[]{:S(2)}) %all-to-all-start.1) | async-done | bytes 458784 | tf_op jit(solution)/shard_map/all_to_all | solution.py:78
  60.7 2.6 fusion.9
  66.2 3.4 all-to-all-start.2
  69.6 2.1 fusion.24
  72.9 6.7 %all-to-all-done.2 = bf16[32,4,8,128]{3,2,1,0:T(8,128)(2,1)S(1)} async-done(((bf16[32,4,8,128]{3,2,1,0:T(8,128)(2,1)}), bf16[32,4,8,128]{3,2,1,0:T(8,128)(2,1)S(1)}, u32[]{:S(2)}, u32[]{:S(2)}) %all-to-all-start.2) | async-done | bytes 262176 | tf_op jit(solution)/shard_map/all_to_all | solution.py:88
  79.6 3.5 all-to-all-start.4
  84.4 2.1 fusion.21
  87.8 6.3 %all-to-all-done.4 = bf16[4,32,14,128]{3,0,2,1:T(4,128)(2,1)S(1)} async-done(((bf16[4,32,14,128]{3,0,2,1:T(4,128)(2,1)}), bf16[4,32,14,128]{3,0,2,1:T(4,128)(2,1)S(1)}, u32[]{:S(2)}, u32[]{:S(2)}) %all-to-all-start.4) | async-done | bytes 458784 | tf_op jit(solution)/shard_map/all_to_all | solution.py:111
  94.1 4.6 all-to-all-start.5
  99.4 1.9 copy.240
  101.3 3.5 multiply_bitcast_fusion
  104.7 5.2 copy.238
  109.9 2.6 multiply_bitcast_fusion.1
  112.5 5.2 copy.233
  120.6 2.6 copy.231
  124.8 2.6 copy.236
  134.2 109.7 %reduce-scatter.2.cloned.1.call-done = f32[8,4,256]{2,0,1:T(8,128)} async-done(((f32[256,4,256]{2,0,1:T(8,128)}), f32[8,4,256]{2,0,1:T(8,128)}) %reduce-scatter.2.cloned.1.call-update) | async-done | bytes 32784 | tf_op jit(solution)/shard_map/reduce_scatter | solution.py:141
  245.3 318.3 %all-reduce.8.cloned.1.call-done = (f32[256,4,448]{2,1,0:T(4,128)}, f32[448,4,448]{2,1,0:T(4,128)}, f32[256,4,448]{2,1,0:T(4,128)}, f32[448,4,448]{2,1,0:T(4,128)}, f32[448,4,256]{2,1,0:T(4,128)}) async-done(((f32[256,4,448]{2,1,0:T(4,128)}, f32[448,4,448]{2,1,0:T(4,128)}, f32[256,4,448]{2,1,0:T(4,128)}, f32[448,4,448]{2,1,0:T(4,128)}, f32[448,4,256]{2,1,0:T(4,128)}), (f32[256,4,448]{2,1,0:T(4,128)}, ...) | async-done | bytes 11927568
  565.1 1.7 constant_dynamic-slice_fusion.1
  (88 shorter events, 33.8 us)
Async XLA Ops:
  7.2 13.9 %copy-start.18 = (bf16[128,1024]{1,0:T(8,128)(2,1)S(1)}, bf16[128,1024]{1,0:T(8,128)(2,1)}, u32[]{:S(2)}) copy-start(bf16[128,1024]{1,0:T(8,128)(2,1)} %param.8) | copy-start | bytes 786436
  7.2 14.1 %copy-start.10 = (bf16[256,4,448]{0,2,1:T(8,128)(2,1)S(1)}, bf16[256,4,448]{0,2,1:T(8,128)(2,1)}, u32[]{:S(2)}) copy-start(bf16[256,4,448]{0,2,1:T(8,128)(2,1)} %param.9) | copy-start | bytes 2752516
  9.4 21.8 %all-to-all-start.3 = ((bf16[4,32,8,128]{3,2,0,1:T(8,128)(2,1)}), bf16[4,32,8,128]{3,2,0,1:T(8,128)(2,1)S(1)}, u32[]{:S(2)}, u32[]{:S(2)}) async-start(bf16[4,32,8,128]{3,2,0,1:T(8,128)(2,1)} %copy.217), calls=%async_computation.3 | async-start | bytes 524288 | tf_op jit(solution)/shard_map/all_to_all | solution.py:101
  22.9 11.8 %copy-start.11 = (bf16[256,4,448]{0,2,1:T(8,128)(2,1)S(1)}, bf16[256,4,448]{0,2,1:T(8,128)(2,1)}, u32[]{:S(2)}) copy-start(bf16[256,4,448]{0,2,1:T(8,128)(2,1)} %param.11) | copy-start | bytes 2752516
  31.3 14.5 %all-to-all-start = ((bf16[32,4,14,128]{3,1,2,0:T(4,128)(2,1)}), bf16[32,4,14,128]{3,1,2,0:T(4,128)(2,1)S(1)}, u32[]{:S(2)}, u32[]{:S(2)}) async-start(bf16[32,4,14,128]{3,1,2,0:T(4,128)(2,1)} %copy.197), calls=%async_computation | async-start | bytes 917504 | tf_op jit(solution)/shard_map/all_to_all | solution.py:74
  45.8 14.6 %all-to-all-start.1 = ((bf16[32,4,14,128]{3,1,2,0:T(4,128)(2,1)}), bf16[32,4,14,128]{3,1,2,0:T(4,128)(2,1)S(1)}, u32[]{:S(2)}, u32[]{:S(2)}) async-start(bf16[32,4,14,128]{3,1,2,0:T(4,128)(2,1)} %copy.204), calls=%async_computation.1 | async-start | bytes 917504 | tf_op jit(solution)/shard_map/all_to_all | solution.py:78
  52.6 10.7 %copy-start.4 = (bf16[8,4,4,14,128]{4,1,3,2,0:T(4,128)(2,1)}, bf16[8,4,4,14,128]{4,1,3,2,0:T(4,128)(2,1)S(1)}, u32[]{:S(2)}) copy-start(bf16[8,4,4,14,128]{4,1,3,2,0:T(4,128)(2,1)S(1)} %copy.198) | copy-start | bytes 1376260
  60.6 3.9 copy-start.6
  60.7 2.7 copy-start.12
  64.6 7.2 %copy-start.13 = (bf16[4,448,128]{2,1,0:T(8,128)(2,1)}, bf16[4,448,128]{2,1,0:T(8,128)(2,1)S(1)}, u32[]{:S(2)}) copy-start(bf16[4,448,128]{2,1,0:T(8,128)(2,1)S(1)} %get-tuple-element.53) | copy-start | bytes 1376260
  64.6 19.8 %copy-start.15 = (bf16[4,448,128]{2,1,0:T(8,128)(2,1)}, bf16[4,448,128]{2,1,0:T(8,128)(2,1)S(1)}, u32[]{:S(2)}) copy-start(bf16[4,448,128]{2,1,0:T(8,128)(2,1)S(1)} %get-tuple-element.54) | copy-start | bytes 1376260
  66.2 13.4 %all-to-all-start.2 = ((bf16[32,4,8,128]{3,2,1,0:T(8,128)(2,1)}), bf16[32,4,8,128]{3,2,1,0:T(8,128)(2,1)S(1)}, u32[]{:S(2)}, u32[]{:S(2)}) async-start(bf16[32,4,8,128]{3,2,1,0:T(8,128)(2,1)} %copy.210), calls=%async_computation.2 | async-start | bytes 524288 | tf_op jit(solution)/shard_map/all_to_all | solution.py:88
  71.7 11.4 %copy-start.19 = (bf16[128,1024]{1,0:T(8,128)(2,1)S(1)}, bf16[128,1024]{1,0:T(8,128)(2,1)}, u32[]{:S(2)}) copy-start(bf16[128,1024]{1,0:T(8,128)(2,1)} %param.15) | copy-start | bytes 786436
  79.6 14.5 %all-to-all-start.4 = ((bf16[4,32,14,128]{3,0,2,1:T(4,128)(2,1)}), bf16[4,32,14,128]{3,0,2,1:T(4,128)(2,1)S(1)}, u32[]{:S(2)}, u32[]{:S(2)}) async-start(bf16[4,32,14,128]{3,0,2,1:T(4,128)(2,1)} %bitcast.31), calls=%async_computation.4 | async-start | bytes 917504 | tf_op jit(solution)/shard_map/all_to_all | solution.py:111
  83.0 160.9 %reduce-scatter.2.cloned.1.call-start = ((), (), s32[]{:S(2)}) async-start(), calls=%async_computation.7 | async-start | bytes 1081344 | tf_op jit(solution)/shard_map/reduce_scatter | solution.py:141
  86.6 12.4 %copy-start.17 = (bf16[4,448,128,1]{2,1,3,0:T(8,128)(2,1)S(1)}, bf16[4,448,128,1]{2,1,3,0:T(8,128)(2,1)}, u32[]{:S(2)}) copy-start(bf16[4,448,128,1]{2,1,3,0:T(8,128)(2,1)} %copy-done.16) | copy-start | bytes 1376260
  94.1 4.6 copy-start.8
  94.1 23.8 %all-to-all-start.5 = ((bf16[4,32,14,128]{3,0,2,1:T(4,128)(2,1)}), bf16[4,32,14,128]{3,0,2,1:T(4,128)(2,1)}, u32[]{:S(2)}, u32[]{:S(2)}) async-start(bf16[4,32,14,128]{3,0,2,1:T(4,128)(2,1)} %bitcast.39), calls=%async_computation.5 | async-start | bytes 917504 | tf_op jit(solution)/shard_map/all_to_all | solution.py:112
  98.7 464.9 %all-reduce.8.cloned.1.call-start = ((), (), s32[]{:S(2)}) async-start(), calls=%async_computation.8 | async-start | bytes 26738688
  104.7 5.2 copy-start.5
  104.7 5.2 copy-start.14
  112.5 5.2 copy-start.9
  127.5 5.0 copy-start.3
  130.0 2.8 copy-start.1
  (6 other events, 7.9 us)
Sparse Core Ops, SparseCore 0:
  86.4 157.4 reduce-scatter.1
  247.3 316.3 all-reduce.7
where the time goes:
time: 576 us; the launch traced here: 575 us
  waiting for transfers between devices  463 us (80%)
  local copies, waits for them, and re-layouts  42.5 us (7%)
  starting transfers between devices  30.4 us (5%)
  matrix products  23 us (4%)
  between operations  15.8 us (3%)
    unnamed x3, waiting for transfers between devices  318 us
    reduce_scatter x1, waiting for transfers between devices, local(): lax.psum_scatter(whole_terms[5], 'dp', scatter_dimension=0, tiled=True)  110 us
    unnamed x54, local copies, waits for them, and re-layouts  14.2 us
    all_to_all x1, starting transfers between devices, local(): lax.all_to_all(down_flow, 'blk', split_axis=1, concat_axis=0, tiled=True)  11.6 us
  transfers between devices with their start and end apart: 8, of which 7 were waited for; matrix products, arithmetic and copies ran while one was open for 9% of the time, Pallas kernels for 0%

commit v1 on v0

v1 whole, which is shorter than its diff:
```python
import types

import jax
import jax.numpy as jnp
import numpy as np
from jax import lax
from jax.experimental import pallas as pl
from jax.experimental.pallas import tpu as pltpu
from jax.sharding import PartitionSpec as P

BF = jnp.bfloat16
F32 = jnp.float32
MESH = pl.DeviceIdType.MESH

NB = 32
KB = 4
DB = 256
MB = 448
MS = 14
T = 128
X, Z, Y = 4, 4, 4
OFFS = ((0, 1), (1, 1), (3, 1), (2, 1), (1, 0), (3, 0), (2, 0))


def permutations():
    pair = np.zeros((448, 448), np.float32)
    for b in range(4):
        for zh in range(2):
            for a in range(4):
                for r in range(MS):
                    pair[((b * 2 + zh) * 4 + a) * MS + r, ((zh * 4 + a) * 4 + b) * MS + r] = 1.0
    spread = np.zeros((2, 256, 448), np.float32)
    twin = np.zeros((2, 2, 256, 256), np.float32)
    for c in range(2):
        for x in range(X):
            for z in range(Z):
                d = z * 8 + x * 2 + c
                for i in range(MS):
                    spread[c, (x * 4 + z) * 16 + i, d * MS + i] = 1.0
                for q in range(2):
                    for i in range(8):
                        twin[q, c, (x * 4 + z) * 16 + q * 8 + i, d * 8 + i] = 1.0
    return (
        np.asarray(pair, jnp.bfloat16),
        np.asarray(spread.reshape(512, 448), jnp.bfloat16),
        np.asarray(twin.reshape(2, 512, 256), jnp.bfloat16),
    )


def nn(a, b):
    return lax.dot_general(a, b, (((1,), (0,)), ((), ())), preferred_element_type=F32)


def nt(a, b):
    return lax.dot_general(a, b, (((1,), (1,)), ((), ())), preferred_element_type=F32)


def tn(a, b):
    return lax.dot_general(a, b, (((0,), (0,)), ((), ())), preferred_element_type=F32)


INPUTS = ("x", "g", "wgr", "wur", "wdl", "pair", "wgl", "wul", "wdr", "spread", "twin")
SHAPES = {
    "x": (T, KB * DB),
    "g": (T, KB * DB),
    "wgr": (KB, MB, DB),
    "wur": (KB, MB, DB),
    "wdl": (KB, DB, DB),
    "pair": (448, 448),
    "wgl": (KB, MB, MB),
    "wul": (KB, MB, MB),
    "wdr": (KB, DB, MB),
    "spread": (512, 448),
    "twin": (2, 512, 256),
}
GROUPS = (("left", 4, 896), ("dright", 4, 256), ("dleft", 2, 256), ("gright", 1, 896), ("uright", 1, 896))
OUTS = ("mixed", "gtok") + tuple("o_" + name for name, _, _ in GROUPS)


def scratch_list():
    out = []

    def add(name, shape, dtype=BF):
        out.append((name, pltpu.VMEM(shape, dtype)))

    for name in INPUTS:
        add("v_" + name, SHAPES[name])
    out.append(("in_sem", pltpu.SemaphoreType.DMA((len(INPUTS),))))
    for name, rows in (("ag", 224), ("au", 224), ("dg", 224), ("du", 224), ("b", 128), ("c", 128)):
        add("s_" + name, (8, rows, T))
        add("r_" + name, (8, rows, T))
        out.append(("ss_" + name, pltpu.SemaphoreType.DMA((7,))))
        out.append(("rs_" + name, pltpu.SemaphoreType.DMA((7,))))
    add("flow", (KB, MB, T), F32)
    for name in ("seen_g", "seen_u", "back_g", "back_u"):
        add(name, (KB, Y, 112, T))
    add("gate_pre", (KB, T, MB), F32)
    add("act", (KB, T, MB), F32)
    add("slope", (KB, T, MB), F32)
    add("hidden", (KB, T, MB))
    add("grad_g", (KB, T, MB))
    add("grad_u", (KB, T, MB))
    add("dback32", (KB, 8, 4, 8, T), F32)
    add("dseen32", (KB, 8, 4, 8, T), F32)
    add("dback", (KB, DB, T))
    add("dseen", (KB, DB, T))
    add("lhs_left", (KB, 2, 256, 256))
    add("rhs_left", (KB, 256, 896))
    add("lhs_dright", (KB, 2, 256, T))
    add("lhs_dleft", (2, 2, 256, 256))
    add("lhs_right", (2, 256, 512))
    add("rhs_gright", (896, 512))
    add("rhs_uright", (896, 512))
    for name, count, lanes in GROUPS:
        add("s0_" + name, (count, 256, lanes))
        add("r0_" + name, (count, 256, lanes))
        add("s1_" + name, (count, X, 64, lanes))
        add("r1_" + name, (count, 3, 64, lanes))
        add("s2_" + name, (count, Z, 16, lanes))
        add("r2_" + name, (3, count, 16, lanes))
        for kind in ("ss0_", "rs0_"):
            out.append((kind + name, pltpu.SemaphoreType.DMA((count,))))
        for kind in ("ss1_", "rs1_"):
            out.append((kind + name, pltpu.SemaphoreType.DMA((count * 3,))))
        for kind in ("ss2_", "rs2_"):
            out.append((kind + name, pltpu.SemaphoreType.DMA((3,))))
    return out


def loop(count, body):
    lax.fori_loop(0, count, lambda i, _: (body(i), 0)[1], 0)


def kernel(scale, names, *refs):
    r = types.SimpleNamespace(**dict(zip(names, refs)))
    v = vars(r)
    dp = lax.axis_index("dp")
    blk = lax.axis_index("blk")
    core, x, z = dp % 2, (dp // 2) % X, dp // 8
    y, zh = blk // 2, blk % 2
    pending = []

    loads = {}
    for i, name in enumerate(INPUTS):
        loads[name] = pltpu.make_async_copy(v["h_" + name], v["v_" + name], r.in_sem.at[i])
        loads[name].start()

    def need(*which):
        for name in which:
            loads[name].wait()

    def blk_peer(dy, dz):
        return ((y + dy) % Y) * 2 + (zh + dz) % 2

    def dp_id(z_, x_, c_):
        return (z_ * 8 + x_ * 2 + c_, blk)

    core_id = dp_id(z, x, 1 - core)
    x_ids = [dp_id(z, (x + d) % X, core) for d in (1, 2, 3)]
    z_ids = [dp_id((z + d) % Z, x, core) for d in (1, 2, 3)]
    everyone = [(dp, blk_peer(dy, dz)) for dy, dz in OFFS] + [core_id] + x_ids + z_ids

    barrier = pltpu.get_barrier_semaphore()
    for who in everyone:
        pl.semaphore_signal(barrier, inc=1, device_id=who, device_id_type=MESH)

    def remote(src, dst, ss, rs, who):
        copy = pltpu.make_async_remote_copy(
            src_ref=src, dst_ref=dst, send_sem=ss, recv_sem=rs, device_id=who, device_id_type=MESH
        )
        copy.start()
        pending.append(copy)
        return copy

    def exchange(name):
        s, d, ss, rs = (v[k + name] for k in ("s_", "r_", "ss_", "rs_"))
        out = {}
        for i, (dy, dz) in enumerate(OFFS):
            p = blk_peer(dy, dz)
            out[dy, dz] = remote(s.at[p], d.at[blk], ss.at[i], rs.at[i], (dp, p))
        d[blk] = s[blk]
        return out

    def slabs(name):
        for p in range(8):
            rows = r.flow[:, p * 56 : (p + 1) * 56, :]
            v["s_" + name][p] = rows.reshape(224, T).astype(BF)

    def unslab(name, copies, out):
        for dy in range(4):
            for dz in range(2):
                if (dy, dz) != (0, 0):
                    copies[dy, dz].wait_recv()
            ys = (y - dy + Y) % Y
            two = v["r_" + name][pl.ds(ys * 2, 2)].reshape(448, T)
            moved = nn(r.v_pair[...], two).astype(BF)
            out[:, pl.ds(ys, 1)] = moved.reshape(KB, 1, 112, T)

    def unswap(name, copies, wide, out):
        for copy in copies.values():
            copy.wait_recv()

        def one(s):
            got = v["r_" + name][s].astype(F32).reshape(4, 4, 8, T)
            for a in range(4):
                for b in range(4):
                    wide[b, s, a] = got[a, b]

        loop(8, one)

        def two(b):
            out[b] = wide[b].reshape(DB, T).astype(BF)

        loop(KB, two)

    def right(weight):
        for k in range(KB):
            r.flow[k] = nt(weight[k], r.v_x[:, k * DB : (k + 1) * DB])

    need("x", "wgr")
    right(r.v_wgr)
    slabs("ag")
    pl.semaphore_wait(barrier, len(everyone))
    from_ag = exchange("ag")
    need("wur")
    right(r.v_wur)
    slabs("au")
    from_au = exchange("au")

    need("g", "wdl")
    for j in range(KB):
        f = nt(r.v_wdl[j], r.v_g[:, j * DB : (j + 1) * DB]).astype(BF)
        r.s_c[:, j * 32 : (j + 1) * 32, :] = f.reshape(8, 32, T)
    from_c = exchange("c")

    need("pair", "spread", "twin")
    r.rhs_gright[...] = jnp.zeros_like(r.rhs_gright)
    r.rhs_uright[...] = jnp.zeros_like(r.rhs_uright)
    for k in range(KB):
        f = nt(r.v_twin[k // 2], r.v_x[:, k * DB : (k + 1) * DB]).astype(BF)
        r.lhs_right[:, :, k * T : (k + 1) * T] = f.reshape(2, 256, T)
    need("wgl", "wul", "wdr")

    unslab("ag", from_ag, r.seen_g)

    def gate(j):
        r.gate_pre[j] = tn(r.seen_g[j].reshape(MB, T), r.v_wgl[j])

    loop(KB, gate)

    unslab("au", from_au, r.seen_u)

    def forward(j):
        up = tn(r.seen_u[j].reshape(MB, T), r.v_wul[j])
        pre = r.gate_pre[j]
        sig = jax.nn.sigmoid(pre)
        act = pre * sig
        hidden = (act * up).astype(BF)
        r.act[j] = act
        r.slope[j] = up * sig * (1.0 + pre * (1.0 - sig))
        r.hidden[j] = hidden
        f = nt(r.v_wdr[j], hidden).astype(BF)
        r.s_b[:, pl.ds(pl.multiple_of(j * 32, 32), 32), :] = f.reshape(8, 32, T)

    loop(KB, forward)
    from_b = exchange("b")

    unswap("c", from_c, r.dback32, r.dback)

    def backward(j):
        hf = tn(r.dback[j], r.v_wdr[j])
        gg = (hf * r.slope[j]).astype(BF)
        ug32 = hf * r.act[j]
        ug = ug32.astype(BF)
        r.grad_g[j] = gg
        r.grad_u[j] = ug
        r.flow[j] = nt(r.v_wgl[j], gg)

    loop(KB, backward)
    slabs("dg")
    from_dg = exchange("dg")

    def backward_up(j):
        r.flow[j] = nt(r.v_wul[j], r.grad_u[j])

    loop(KB, backward_up)
    slabs("du")
    from_du = exchange("du")

    moves = {}

    def start_core(name, count, half):
        s0, r0, ss, rs = (v[k + name] for k in ("s0_", "r0_", "ss0_", "rs0_"))
        for j in range(count):
            s0[j] = half(j, 1 - core).astype(BF)
            moves[name, 0, j] = remote(s0.at[j], r0.at[j], ss.at[j], rs.at[j], core_id)

    def start_x(name, count, half):
        r0, s1, r1, ss, rs = (v[k + name] for k in ("r0_", "s1_", "r1_", "ss1_", "rs1_"))
        for j in range(count):
            own = half(j, core)
            moves[name, 0, j].wait_recv()
            s1[j] = (own + r0[j].astype(F32)).astype(BF).reshape(s1.shape[1:])
            for i in (0, 2, 1):
                moves[name, 1, j, i] = remote(
                    s1.at[j, (x + i + 1) % X],
                    r1.at[j, i],
                    ss.at[j * 3 + i],
                    rs.at[j * 3 + i],
                    x_ids[i],
                )

    def start_z(name, count):
        s1, r1, s2, r2, ss, rs = (
            v[k + name] for k in ("s1_", "r1_", "s2_", "r2_", "ss2_", "rs2_")
        )
        for j in range(count):
            for i in range(3):
                moves[name, 1, j, i].wait_recv()
            total = s1[j, x].astype(F32)
            for i in range(3):
                total = total + r1[j, i].astype(F32)
            s2[j] = total.astype(BF).reshape(s2.shape[1:])
        for i in range(3):
            moves[name, 2, i] = remote(
                s2.at[:, (z + i + 1) % Z], r2.at[i], ss.at[i], rs.at[i], z_ids[i]
            )

    def finish(name, count):
        s2, r2, out = v["s2_" + name], v["r2_" + name], v["o_" + name]
        for i in range(3):
            moves[name, 2, i].wait_recv()
        for j in range(count):
            total = s2[j, z].astype(F32)
            for i in range(3):
                total = total + r2[i, j].astype(F32)
            out[j] = scale * total

    def sides(j):
        f = nn(r.v_spread[...], r.seen_g[j].reshape(MB, T)).astype(BF)
        r.lhs_left[j, :, :, :T] = f.reshape(2, 256, T)
        f = nn(r.v_spread[...], r.seen_u[j].reshape(MB, T)).astype(BF)
        r.lhs_left[j, :, :, T:] = f.reshape(2, 256, T)
        f = nt(r.v_spread[...], r.hidden[j]).astype(BF)
        r.lhs_dright[j] = f.reshape(2, 256, T)
        gate_part = jnp.concatenate([r.grad_g[j], jnp.zeros((T, 448), BF)], axis=1)
        up_part = jnp.concatenate([jnp.zeros((T, 448), BF), r.grad_u[j]], axis=1)
        r.rhs_left[j, :T, :] = gate_part
        r.rhs_left[j, T:, :] = up_part

    loop(KB, sides)

    def left_half(j, c):
        return nn(r.lhs_left[j, c], r.rhs_left[j])

    def dright_half(j, c):
        return nt(r.lhs_dright[j, c], r.dback[j])

    def dleft_half(q, c):
        rows = [r.v_g[:, (2 * q + i) * DB : (2 * q + i + 1) * DB] for i in range(2)]
        return nn(r.lhs_dleft[q, c], jnp.concatenate(rows, axis=0))

    start_core("left", 4, left_half)
    start_core("dright", 4, dright_half)
    start_x("left", 4, left_half)
    start_x("dright", 4, dright_half)

    unswap("b", from_b, r.dseen32, r.dseen)
    for j in range(KB):
        r.mixed[:, j * DB : (j + 1) * DB] = tn(r.dseen[j], r.v_wdl[j]).astype(BF)
        f = nn(r.v_twin[j % 2], r.dseen[j]).astype(BF)
        r.lhs_dleft[j // 2, :, :, (j % 2) * T : (j % 2 + 1) * T] = f.reshape(2, 256, T)
    start_core("dleft", 2, dleft_half)
    start_x("dleft", 2, dleft_half)

    def spread_back(back, rhs):
        for k in range(KB):
            q, i = k // 2, k % 2
            rhs[i * MB : (i + 1) * MB, k * T : (k + 1) * T] = back[k].reshape(MB, T)

    def gright_half(j, c):
        return nt(r.lhs_right[c], r.rhs_gright[...])

    def uright_half(j, c):
        return nt(r.lhs_right[c], r.rhs_uright[...])

    unslab("dg", from_dg, r.back_g)
    spread_back(r.back_g, r.rhs_gright)
    start_core("gright", 1, gright_half)
    start_x("gright", 1, gright_half)
    start_z("left", 4)
    start_z("dright", 4)
    start_z("dleft", 2)

    unslab("du", from_du, r.back_u)
    spread_back(r.back_u, r.rhs_uright)
    start_core("uright", 1, uright_half)
    start_x("uright", 1, uright_half)

    for k in range(KB):
        total = tn(r.back_g[k].reshape(MB, T), r.v_wgr[k])
        total = total + tn(r.back_u[k].reshape(MB, T), r.v_wur[k])
        r.gtok[:, k * DB : (k + 1) * DB] = total.astype(BF)

    start_z("gright", 1)
    finish("left", 4)
    finish("dright", 4)
    finish("dleft", 2)
    start_z("uright", 1)
    finish("gright", 1)
    finish("uright", 1)
    for copy in pending:
        copy.wait_send()


def local(tokens, gate_right, gate_left, upward_right, upward_left, down_right, down_left, cotangent):
    scale = float(tokens.shape[0] * lax.axis_size("dp")) ** (-0.5)
    pair, spread, twin = permutations()
    given = {
        "x": tokens,
        "g": cotangent,
        "wgr": jnp.transpose(gate_right, (1, 2, 0)),
        "wur": jnp.transpose(upward_right, (1, 2, 0)),
        "wdl": jnp.transpose(down_left, (1, 0, 2)),
        "pair": jnp.asarray(pair),
        "wgl": jnp.transpose(gate_left, (1, 0, 2)),
        "wul": jnp.transpose(upward_left, (1, 0, 2)),
        "wdr": jnp.transpose(down_right, (1, 2, 0)),
        "spread": jnp.asarray(spread),
        "twin": jnp.asarray(twin),
    }
    scratch = scratch_list()
    names = ["h_" + name for name in INPUTS] + list(OUTS) + [name for name, _ in scratch]
    shapes = [jax.ShapeDtypeStruct((T, KB * DB), BF)] * 2
    shapes += [jax.ShapeDtypeStruct((count, 16, lanes), F32) for _, count, lanes in GROUPS]

    def body(*refs):
        kernel(scale, names, *refs)

    mixed, gtok, left, dright, dleft, gright, uright = pl.pallas_call(
        body,
        out_shape=shapes,
        in_specs=[pl.BlockSpec(memory_space=pl.ANY)] * len(INPUTS),
        out_specs=[pl.BlockSpec(memory_space=pltpu.VMEM)] * len(OUTS),
        scratch_shapes=[shape for _, shape in scratch],
        compiler_params=pltpu.CompilerParams(
            collective_id=0, has_side_effects=True, vmem_limit_bytes=58 * 1024 * 1024
        ),
        name="monarch",
    )(*[given[name] for name in INPUTS])

    left = jnp.transpose(left[:, :MS, :], (1, 0, 2))
    dright = jnp.transpose(dright[:, :MS, :], (1, 0, 2))
    dleft = dleft.reshape(2, 2, 8, DB).transpose(2, 0, 1, 3).reshape(8, KB, DB)

    def unpack(right):
        return right.reshape(2, 8, 2, MB).transpose(1, 0, 2, 3).reshape(8, KB, MB)

    return (
        mixed,
        gtok,
        unpack(gright),
        left[:, :, :MB],
        unpack(uright),
        left[:, :, MB:],
        dright,
        dleft,
    )


def solution(mesh):
    weight = P(None, "blk", None)
    grad = P("dp", "blk", None)
    return jax.shard_map(
        local,
        mesh=mesh,
        in_specs=(P("dp", "blk"),) + (weight,) * 6 + (P("dp", "blk"),),
        out_specs=(P("dp", "blk"),) * 2 + (grad,) * 6,
        check_vma=False,
    )
```

time: 576 us -> 118 us (0.20)
  waiting for transfers between devices: 463 us -> 0 us
  Pallas kernels: 0 us -> 98.3 us
  starting transfers between devices: 30.4 us -> 0 us
  local copies, waits for them, and re-layouts: 42.5 us -> 18.5 us
  matrix products: 23 us -> 0 us
  between operations: 15.8 us -> 0.72 us
    unnamed x3 -> x0, waiting for transfers between devices: 318 us -> none
    reduce_scatter x1 -> x0, waiting for transfers between devices: 110 us -> none  [local(): lax.psum_scatter(whole_terms[5], 'dp', scatter_dimension=0, tiled=True)]
    pallas_call x0 -> x1, Pallas kernels: none -> 98.3 us  [local(): pl.pallas_call(body, out_shape=shapes, in_specs=[pl.BlockSpec(memory_spac...]
    all_to_all x6 -> x0, waiting for transfers between devices: 35.3 us -> none  [the longest x1 7.81 us: local(): lax.all_to_all(upward_mixed, 'blk', split_axis=0, concat_axis=1, tiled=True)]
    all_to_all x6 -> x0, starting transfers between devices: 30.1 us -> none  [the longest x1 11.6 us: local(): lax.all_to_all(down_flow, 'blk', split_axis=1, concat_axis=0, tiled=True)]
    dot_general x18 -> x0, matrix products: 23 us -> none  [the longest x2 6.04 us: term_left(): jnp.einsum('jmt,jnt->mjn', seen, gradient, preferred_element_type=jnp.flo...]
    mul x7 -> x0, local copies, waits for them, and re-layouts: 19.8 us -> none  [the longest x2 10.3 us: term_left(): grad_scale * jnp.einsum('jmt,jnt->mjn', seen, gradient, preferred_element...]
    unnamed x54 -> x13, local copies, waits for them, and re-layouts: 14.2 us -> 7.93 us
  transfers between devices with their start and end apart: 8 -> 0, of which waited for: 7 -> 0; matrix products, arithmetic and copies ran while one was open for 9% -> 0% of each run, Pallas kernels for 0% -> 0%
where the time goes in v1:
time: 118 us
  Pallas kernels  98.3 us (83%)
  local copies, waits for them, and re-layouts  18.5 us (16%)
    pallas_call x1, Pallas kernels, local(): pl.pallas_call(body, out_shape=shapes, in_specs=[pl.BlockSpec(memory_spac...  98.3 us
    unnamed x13, local copies, waits for them, and re-layouts  7.93 us
    transpose x1, local copies, waits for them, and re-layouts, local(): jnp.transpose(upward_left, (1, 0, 2))  4.04 us
    reshape x4, local copies, waits for them, and re-layouts, unpack(): return right.reshape(2, 8, 2, MB).transpose(1, 0, 2, 3).reshape(8, KB, MB)  3.23 us

profile of v1, /device:TPU:1, one launch (start us, length us, event | category | flops | bytes accessed | tf_op | source)
XLA Modules:
  0.0 117.6 jit_solution(1745701735072723197)
XLA Ops:
  0.6 0.0 copy-start
  0.6 2.1 %copy.33 = bf16[256,4,256]{2,0,1:T(8,128)(2,1)} copy(bf16[256,4,256]{2,1,0:T(4,128)(2,1)} %param.17) | data formatting | bytes 1048576 | tf_op args[6]
  2.7 2.4 %copy.22 = bf16[448,4,256]{0,2,1:T(8,128)(2,1)} copy(bf16[448,4,256]{2,1,0:T(4,128)(2,1)} %param.16) | data formatting | bytes 1835008 | tf_op args[5]
  5.0 0.0 copy-done
  5.0 4.0 %copy_bitcast_fusion = (bf16[4,448,448]{2,1,0:T(8,128)(2,1)}, bf16[4,448,448]{2,1,0:T(8,128)(2,1)}) fusion(bf16[448,4,448]{2,1,0:T(4,128)(2,1)S(1)} %copy-done, bf16[448,4,448]{2,1,0:T(4,128)(2,1)} %param.13), kind=kLoop, calls=%fused_computation | loop fusion | bytes 6422528 | tf_op jit(solution)/shard_map/transpose | solution.py:427
  9.1 98.3 %monarch.1 = (bf16[128,1024]{1,0:T(8,128)(2,1)}, bf16[128,1024]{1,0:T(8,128)(2,1)}, f32[4,16,896]{2,1,0:T(8,128)}, f32[4,16,256]{2,1,0:T(8,128)}, f32[2,16,256]{...) custom-call(bf16[128,1024]{1,0:T(8,128)(2,1)} %refs_0_.1, bf16[128,1024]{1,0:T(8,128)(2,1)} %refs_1_.1, ...), custom_call_target="tpu_custom_call" | custom-call | tf_op jit(solution)/shard_map/monarch/pallas_call | solution.py:440
  107.4 0.0 copy-start.2
  107.4 0.0 copy-start.1
  107.4 1.4 %copy.29 = f32[8,4,256]{2,1,0:T(4,128)} copy(f32[8,4,256]{2,0,1:T(8,128)} %bitcast.27) | data formatting | bytes 65536 | tf_op jit(solution)/shard_map/reshape | solution.py:454
  108.9 0.9 reshape.34
  109.8 0.7 reshape.35
  110.5 0.9 reshape.36
  111.4 0.7 reshape.37
  112.1 0.8 slice_bitcast_fusion.1
  113.0 0.7 copy.28
  113.6 1.0 slice_bitcast_fusion
  114.6 0.1 fusion
  114.7 0.7 copy.27
  115.4 0.7 copy.26
  116.1 0.0 copy-done.2
  116.1 0.7 copy.36
  116.8 0.0 copy-done.1
  116.8 0.7 copy.37
  (2 shorter events, 0.0 us)
Async XLA Ops:
  0.6 4.4 %copy-start = (bf16[448,4,448]{2,1,0:T(4,128)(2,1)S(1)}, bf16[448,4,448]{2,1,0:T(4,128)(2,1)}, u32[]{:S(2)}) copy-start(bf16[448,4,448]{2,1,0:T(4,128)(2,1)} %param.15) | copy-start | bytes 4816900
  107.4 8.8 %copy-start.2 = (bf16[128,1024]{1,0:T(8,128)(2,1)S(1)}, bf16[128,1024]{1,0:T(8,128)(2,1)}, u32[]{:S(2)}) copy-start(bf16[128,1024]{1,0:T(8,128)(2,1)} %get-tuple-element.42) | copy-start | bytes 786436
  107.4 9.4 %copy-start.1 = (bf16[128,1024]{1,0:T(8,128)(2,1)S(1)}, bf16[128,1024]{1,0:T(8,128)(2,1)}, u32[]{:S(2)}) copy-start(bf16[128,1024]{1,0:T(8,128)(2,1)} %get-tuple-element.43) | copy-start | bytes 786436

commit v2 on v1

v2 whole, which is shorter than its diff:
```python
import types

import jax
import jax.numpy as jnp
import numpy as np
from jax import lax
from jax.experimental import pallas as pl
from jax.experimental.pallas import tpu as pltpu
from jax.sharding import PartitionSpec as P

BF = jnp.bfloat16
F32 = jnp.float32
MESH = pl.DeviceIdType.MESH

NB = 32
KB = 4
DB = 256
MB = 448
MS = 14
T = 128
VMEM_LIMIT = 60 * 1024 * 1024
X, Z, Y = 4, 4, 4
OFFS = ((0, 1), (1, 1), (3, 1), (2, 1), (1, 0), (3, 0), (2, 0))


def permutations():
    take = np.zeros((224, 224), np.float32)
    meet = np.zeros((224, 224), np.float32)
    back = np.zeros((224, 224), np.float32)
    for k in range(4):
        for h in range(2):
            for j in range(2):
                for r in range(MS):
                    take[((h * 4 + k) * 2 + j) * MS + r, ((k * 2 + h) * 2 + j) * MS + r] = 1.0
                    meet[((j * 2 + h) * 4 + k) * MS + r, ((h * 4 + k) * 2 + j) * MS + r] = 1.0
                    back[((k * 2 + h) * 2 + j) * MS + r, ((h * 2 + j) * 4 + k) * MS + r] = 1.0
    turn = np.zeros((448, 448), np.float32)
    for p in range(8):
        for h in range(2):
            for i in range(2 * MS):
                turn[h * 224 + p * 28 + i, p * 56 + h * 28 + i] = 1.0
    spread = np.zeros((2, 256, 448), np.float32)
    order = np.zeros((2, 128, 256), np.float32)
    twin = np.zeros((2, 2, 256, 256), np.float32)
    for c in range(2):
        for x in range(X):
            for z in range(Z):
                d = z * 8 + x * 2 + c
                for i in range(MS):
                    spread[c, (x * 4 + z) * 16 + i, d * MS + i] = 1.0
                for i in range(8):
                    order[c, (x * 4 + z) * 8 + i, d * 8 + i] = 1.0
                    for q in range(2):
                        twin[q, c, (x * 4 + z) * 16 + q * 8 + i, d * 8 + i] = 1.0
    out = {
        "take": take,
        "meet": meet,
        "back": back,
        "turn": turn,
        "spread": spread.reshape(512, 448),
        "order": order.reshape(256, 256),
        "twin": twin.reshape(2, 512, 256),
    }
    return {name: np.asarray(value, jnp.bfloat16) for name, value in out.items()}


def untangle():
    out = np.zeros((2, 256, 448), np.float32)
    for h in range(2):
        for p in range(8):
            for i in range(2 * MS):
                out[h, p * 28 + i, p * 56 + h * 28 + i] = 1.0
    return out


def nn(a, b):
    return lax.dot_general(a, b, (((1,), (0,)), ((), ())), preferred_element_type=F32)


def nt(a, b):
    return lax.dot_general(a, b, (((1,), (1,)), ((), ())), preferred_element_type=F32)


def tn(a, b):
    return lax.dot_general(a, b, (((0,), (0,)), ((), ())), preferred_element_type=F32)


INPUTS = (
    "x",
    "wgr",
    "wur",
    "take",
    "wdl",
    "g",
    "wgl",
    "wul",
    "wdr",
    "meet",
    "order",
    "turn",
    "back",
    "spread",
    "twin",
)
SHAPES = {
    "x": (T, KB * DB),
    "g": (T, KB * DB),
    "wgr": (KB, MB, DB),
    "wur": (KB, MB, DB),
    "wdl": (DB, KB, DB),
    "wgl": (MB, KB, MB),
    "wul": (MB, KB, MB),
    "wdr": (MB, KB, DB),
    "take": (224, 224),
    "meet": (224, 224),
    "back": (224, 224),
    "turn": (448, 448),
    "spread": (512, 448),
    "order": (256, 256),
    "twin": (2, 512, 256),
}
GROUPS = (
    ("left", 4, 896),
    ("dright", 4, 256),
    ("dleft", 2, 256),
    ("right0", 1, 896),
    ("right1", 1, 896),
)
UNPACKED = ("left", "dright", "dleft", "right0", "right1", "columns")
OUTS = ("mixed", "gtok") + tuple("o_" + name for name, _, _ in GROUPS)
SLABS = (
    ("a0", (112, 256)),
    ("a1", (112, 256)),
    ("d0", (112, 256)),
    ("d1", (112, 256)),
    ("b0", (64, T)),
    ("b1", (64, T)),
    ("c", (128, T)),
)


def scratch_list():
    out = []

    def add(name, shape, dtype=BF):
        out.append((name, pltpu.VMEM(shape, dtype)))

    for name in INPUTS:
        add("v_" + name, SHAPES[name])
    out.append(("in_sem", pltpu.SemaphoreType.DMA((len(INPUTS),))))
    for name, slab in SLABS:
        add("s_" + name, (8,) + slab)
        add("r_" + name, (8,) + slab)
        out.append(("ss_" + name, pltpu.SemaphoreType.DMA((7,))))
        out.append(("rs_" + name, pltpu.SemaphoreType.DMA((7,))))
    add("gl", (KB, MB, MB))
    add("ul", (KB, MB, MB))
    add("dr", (KB, DB, MB))
    add("dl", (KB, DB, DB))
    add("turned_g", (KB, 2, 224, DB))
    add("turned_u", (KB, 2, 224, DB))
    add("flow", (KB, MB, 2 * T), F32)
    add("seen", (KB, Y, 112, 2 * T))
    add("back32", (KB, Y, 56, 2 * T), F32)
    add("back", (KB, 224, 2 * T))
    add("act", (KB, T, MB), F32)
    add("slope", (KB, T, MB), F32)
    add("hidden", (KB, T, MB))
    add("dback32", (KB, 8, 4, 8, T), F32)
    add("dseen32", (KB, 8, 4, 8, T), F32)
    add("dback", (KB, DB, T))
    add("dseen", (KB, DB, T))
    add("lhs_left", (KB, 2, 256, 256))
    add("rhs_left", (KB, 256, 896))
    add("lhs_dright", (KB, 2, 256, T))
    add("lhs_dleft", (2, 2, 256, 256))
    add("lhs_right", (2, 128, 512))
    add("rhs_gright", (896, 512))
    add("rhs_uright", (896, 512))
    add("tok", (T, KB * DB), F32)
    for name, count, lanes in GROUPS:
        add("s0_" + name, (count, 256, lanes))
        add("r0_" + name, (count, 256, lanes))
        add("s1_" + name, (count, X, 64, lanes))
        add("r1_" + name, (count, 3, 64, lanes))
        add("s2_" + name, (count, Z, 16, lanes))
        add("r2_" + name, (3, count, 16, lanes))
        for kind in ("ss0_", "rs0_"):
            out.append((kind + name, pltpu.SemaphoreType.DMA((count,))))
        for kind in ("ss1_", "rs1_"):
            out.append((kind + name, pltpu.SemaphoreType.DMA((count * 3,))))
        for kind in ("ss2_", "rs2_"):
            out.append((kind + name, pltpu.SemaphoreType.DMA((3,))))
    return out


def loop(count, body):
    lax.fori_loop(0, count, lambda i, _: (body(i), 0)[1], 0)


def kernel(scale, names, *refs):
    r = types.SimpleNamespace(**dict(zip(names, refs)))
    v = vars(r)
    dp = lax.axis_index("dp")
    blk = lax.axis_index("blk")
    core, x, z = dp % 2, (dp // 2) % X, dp // 8
    y, zh = blk // 2, blk % 2
    pending = []

    loads = {}
    for i, name in enumerate(INPUTS):
        loads[name] = pltpu.make_async_copy(v["h_" + name], v["v_" + name], r.in_sem.at[i])
        loads[name].start()

    def need(*which):
        for name in which:
            loads[name].wait()

    def blk_peer(dy, dz):
        return ((y + dy) % Y) * 2 + (zh + dz) % 2

    def dp_id(z_, x_, c_):
        return (z_ * 8 + x_ * 2 + c_, blk)

    core_id = dp_id(z, x, 1 - core)
    x_ids = [dp_id(z, (x + d) % X, core) for d in (1, 2, 3)]
    z_ids = [dp_id((z + d) % Z, x, core) for d in (1, 2, 3)]
    everyone = [(dp, blk_peer(dy, dz)) for dy, dz in OFFS] + [core_id] + x_ids + z_ids

    barrier = pltpu.get_barrier_semaphore()
    for who in everyone:
        pl.semaphore_signal(barrier, inc=1, device_id=who, device_id_type=MESH)

    def remote(src, dst, ss, rs, who):
        copy = pltpu.make_async_remote_copy(
            src_ref=src, dst_ref=dst, send_sem=ss, recv_sem=rs, device_id=who, device_id_type=MESH
        )
        copy.start()
        pending.append(copy)
        return copy

    def exchange(name):
        s, d, ss, rs = (v[k + name] for k in ("s_", "r_", "ss_", "rs_"))
        out = {}
        for i, (dy, dz) in enumerate(OFFS):
            p = blk_peer(dy, dz)
            out[dy, dz] = remote(s.at[p], d.at[blk], ss.at[i], rs.at[i], (dp, p))
        d[blk] = s[blk]
        return out

    def pairs(name, copies, matrix, use):
        for dy in range(4):
            for dz in range(2):
                if (dy, dz) != (0, 0):
                    copies[dy, dz].wait_recv()
            ys = (y - dy + Y) % Y
            two = v["r_" + name][pl.ds(ys * 2, 2)].reshape(224, 2 * T)
            use(ys, nn(matrix[...], two))

    def unswap(source, wide, out):
        def one(s):
            got = source(s).astype(F32).reshape(4, 4, 8, T)
            for a in range(4):
                for b in range(4):
                    wide[b, s, a] = got[a, b]

        loop(8, one)
        for b in range(KB):
            out[b] = wide[b].reshape(DB, T).astype(BF)

    def arrived(copies):
        for copy in copies.values():
            copy.wait_recv()

    def sent(copies):
        for copy in copies.values():
            copy.wait_send()
        gone = {id(copy) for copy in copies.values()}
        pending[:] = [copy for copy in pending if id(copy) not in gone]

    need("x", "wgr", "wur", "take")
    for k in range(KB):
        xk = r.v_x[:, k * DB : (k + 1) * DB]
        r.flow[k, :, :T] = nt(r.v_wgr[k], xk)
        r.flow[k, :, T:] = nt(r.v_wur[k], xk)
    for p in range(8):
        rows = r.flow[:, p * 56 : (p + 1) * 56, :].reshape(224, 2 * T).astype(BF)
        taken = nn(r.v_take[...], rows).astype(BF)
        r.s_a0[p] = taken[:112]
        r.s_a1[p] = taken[112:]
    pl.semaphore_wait(barrier, len(everyone))
    from_a = [exchange("a0")]

    need("wdl", "g")
    r.dl[...] = jnp.swapaxes(r.v_wdl[...], 0, 1)
    for j in range(KB):
        f = nt(r.dl[j], r.v_g[:, j * DB : (j + 1) * DB]).astype(BF)
        r.s_c[:, j * 32 : (j + 1) * 32, :] = f.reshape(8, 32, T)

    need("wgl", "wul", "wdr", "meet", "order", "turn", "back", "spread", "twin")
    r.gl[...] = jnp.swapaxes(r.v_wgl[...], 0, 1)
    r.ul[...] = jnp.swapaxes(r.v_wul[...], 0, 1)
    eye = lax.broadcasted_iota(jnp.int32, (DB, DB), 0) == lax.broadcasted_iota(jnp.int32, (DB, DB), 1)
    eye = eye.astype(F32).astype(BF)
    swapped = jnp.swapaxes(r.v_wdr[...], 0, 1)
    for k in range(KB):
        r.dr[k] = nt(eye, swapped[k]).astype(BF)
    r.rhs_gright[...] = jnp.zeros_like(r.rhs_gright)
    r.rhs_uright[...] = jnp.zeros_like(r.rhs_uright)
    for k in range(KB):
        f = nt(r.v_order[...], r.v_x[:, k * DB : (k + 1) * DB]).astype(BF)
        r.lhs_right[:, :, k * T : (k + 1) * T] = f.reshape(2, 128, T)

    def turned(k):
        r.turned_g[k] = nn(r.v_turn[...], r.v_wgr[k]).astype(BF).reshape(2, 224, DB)
        r.turned_u[k] = nn(r.v_turn[...], r.v_wur[k]).astype(BF).reshape(2, 224, DB)

    loop(KB, turned)

    def forward(h):
        def keep(ys, moved):
            r.seen[2 * h : 2 * h + 2, pl.ds(ys, 1)] = moved.astype(BF).reshape(2, 1, 112, 2 * T)

        pairs("a%d" % h, from_a[h], r.v_meet, keep)
        for i in range(2):
            j = 2 * h + i
            seen = r.seen[j].reshape(MB, 2 * T)
            pre = tn(seen[:, :T], r.gl[j])
            up = tn(seen[:, T:], r.ul[j])
            sig = jax.nn.sigmoid(pre)
            act = pre * sig
            hidden = (act * up).astype(BF)
            r.act[j] = act
            r.slope[j] = up * sig * (1.0 + pre * (1.0 - sig))
            r.hidden[j] = hidden
            f = nt(r.dr[j], hidden).astype(BF)
            v["s_b%d" % h][:, i * 32 : (i + 1) * 32, :] = f.reshape(8, 32, T)

    def backward(h):
        for i in range(2):
            j = 2 * h + i
            hf = tn(r.dback[j], r.dr[j])
            gg = (hf * r.slope[j]).astype(BF)
            ug = (hf * r.act[j]).astype(BF)
            r.flow[i, :, :T] = nt(r.gl[j], gg)
            r.flow[i, :, T:] = nt(r.ul[j], ug)
            r.rhs_left[j, :T, :] = jnp.concatenate([gg, jnp.zeros((T, MB), BF)], axis=1)
            r.rhs_left[j, T:, :] = jnp.concatenate([jnp.zeros((T, MB), BF), ug], axis=1)
        for p in range(8):
            rows = r.flow[:2, p * 56 : (p + 1) * 56, :].reshape(112, 2 * T)
            v["s_d%d" % h][p] = rows.astype(BF)

    moves = {}

    def start_core(name, which, half):
        s0, r0, ss, rs = (v[k + name] for k in ("s0_", "r0_", "ss0_", "rs0_"))
        for j in which:
            s0[j] = half(j, 1 - core).astype(BF)
            moves[name, 0, j] = remote(s0.at[j], r0.at[j], ss.at[j], rs.at[j], core_id)

    def start_x(name, which, half):
        r0, s1, r1, ss, rs = (v[k + name] for k in ("r0_", "s1_", "r1_", "ss1_", "rs1_"))
        for j in which:
            own = half(j, core)
            moves[name, 0, j].wait_recv()
            s1[j] = (own + r0[j].astype(F32)).astype(BF).reshape(s1.shape[1:])
            for i in (0, 2, 1):
                moves[name, 1, j, i] = remote(
                    s1.at[j, (x + i + 1) % X],
                    r1.at[j, i],
                    ss.at[j * 3 + i],
                    rs.at[j * 3 + i],
                    x_ids[i],
                )

    def start_z(name, count):
        s1, r1, s2, r2, ss, rs = (
            v[k + name] for k in ("s1_", "r1_", "s2_", "r2_", "ss2_", "rs2_")
        )
        for j in range(count):
            for i in range(3):
                moves[name, 1, j, i].wait_recv()
            total = s1[j, x].astype(F32)
            for i in range(3):
                total = total + r1[j, i].astype(F32)
            s2[j] = total.astype(BF).reshape(s2.shape[1:])
        for i in range(3):
            moves[name, 2, i] = remote(
                s2.at[:, (z + i + 1) % Z], r2.at[i], ss.at[i], rs.at[i], z_ids[i]
            )

    def finish(name, count):
        s2, r2, out = v["s2_" + name], v["r2_" + name], v["o_" + name]
        for i in range(3):
            moves[name, 2, i].wait_recv()
        for j in range(count):
            total = s2[j, z].astype(F32)
            for i in range(3):
                total = total + r2[i, j].astype(F32)
            out[j] = scale * total

    def sides(h):
        for j in (2 * h, 2 * h + 1):
            f = nn(r.v_spread[...], r.seen[j].reshape(MB, 2 * T)).astype(BF)
            r.lhs_left[j] = f.reshape(2, 256, 2 * T)
            f = nt(r.v_spread[...], r.hidden[j]).astype(BF)
            r.lhs_dright[j] = f.reshape(2, 256, T)

    def left_half(j, c):
        return nn(r.lhs_left[j, c], r.rhs_left[j])

    def dright_half(j, c):
        return nt(r.lhs_dright[j, c], r.dback[j])

    def dleft_half(q, c):
        rows = [r.v_g[:, (2 * q + i) * DB : (2 * q + i + 1) * DB] for i in range(2)]
        return nn(r.lhs_dleft[q, c], jnp.concatenate(rows, axis=0))

    def right_half(j, c):
        both = [nt(r.lhs_right[c], rhs[...]) for rhs in (r.rhs_gright, r.rhs_uright)]
        both = [part.reshape(16, 1, 8, 896) for part in both]
        return jnp.concatenate(both, axis=1).reshape(256, 896)

    def token_part(h, k):
        part = tn(r.back[k, :, :T], r.turned_g[k, h])
        return part + tn(r.back[k, :, T:], r.turned_u[k, h])

    def right(h):
        def keep(ys, moved):
            r.back32[:, pl.ds(ys, 1)] = moved.reshape(KB, 1, 56, 2 * T)

        pairs("d%d" % h, from_d[h], r.v_back, keep)
        for k in range(KB):
            back = r.back32[k].reshape(224, 2 * T).astype(BF)
            r.back[k] = back
            r.rhs_gright[k * 224 : (k + 1) * 224, k * T : (k + 1) * T] = back[:, :T]
            r.rhs_uright[k * 224 : (k + 1) * 224, k * T : (k + 1) * T] = back[:, T:]
        start_core("right%d" % h, (0,), right_half)

    def left(h):
        which = (2 * h, 2 * h + 1)
        sides(h)
        start_core("left", which, left_half)
        start_core("dright", which, dright_half)
        start_x("left", which, left_half)
        start_x("dright", which, dright_half)

    sent(from_a[0])
    from_c = exchange("c")
    forward(0)
    sent(from_c)
    from_a.append(exchange("a1"))
    arrived(from_c)
    unswap(lambda s: r.r_c[s], r.dback32, r.dback)
    backward(0)
    left(0)
    sent(from_a[1])
    from_d = [exchange("d0")]
    forward(1)
    backward(1)
    left(1)
    sent(from_d[0])
    from_d.append(exchange("d1"))

    right(0)
    for k in range(KB):
        r.tok[:, k * DB : (k + 1) * DB] = token_part(0, k)
    start_x("right0", (0,), right_half)
    sent(from_d[1])
    from_b = [exchange("b0"), exchange("b1")]

    right(1)
    start_x("right1", (0,), right_half)
    start_z("left", 4)
    start_z("dright", 4)
    start_z("right0", 1)

    for copies in from_b:
        arrived(copies)
    unswap(lambda s: jnp.concatenate([r.r_b0[s], r.r_b1[s]], axis=0), r.dseen32, r.dseen)
    for j in range(KB):
        f = nn(r.v_twin[j % 2], r.dseen[j]).astype(BF)
        r.lhs_dleft[j // 2, :, :, (j % 2) * T : (j % 2 + 1) * T] = f.reshape(2, 256, T)
    start_core("dleft", (0, 1), dleft_half)
    start_x("dleft", (0, 1), dleft_half)
    for k in range(KB):
        columns = slice(k * DB, (k + 1) * DB)
        r.gtok[:, columns] = (r.tok[:, columns] + token_part(1, k)).astype(BF)
    start_z("right1", 1)
    for j in range(KB):
        r.mixed[:, j * DB : (j + 1) * DB] = tn(r.dseen[j], r.dl[j]).astype(BF)
    start_z("dleft", 2)
    finish("left", 4)
    finish("dright", 4)
    finish("right0", 1)
    finish("right1", 1)
    finish("dleft", 2)
    for copy in pending:
        copy.wait_send()


def unpack(names, *refs):
    r = types.SimpleNamespace(**dict(zip(names, refs)))
    copies = [
        pltpu.make_async_copy(r.mixed_in, r.mixed, r.sem.at[0]),
        pltpu.make_async_copy(r.gtok_in, r.gtok, r.sem.at[1]),
    ]
    for i, name in enumerate(UNPACKED):
        copies.append(pltpu.make_async_copy(vars(r)["h_" + name], vars(r)[name], r.sem.at[2 + i]))
    for copy in copies:
        copy.start()
    for copy in copies[2:]:
        copy.wait()
    total = None
    for h, source in enumerate((r.right0, r.right1)):
        rows = source[0]
        parts = [rows[:, :256]] + [pltpu.roll(rows, 896 - 224 * k, 1)[:, :256] for k in (1, 2, 3)]
        part = lax.dot_general(
            jnp.concatenate(parts, axis=0),
            r.columns[h],
            (((1,), (0,)), ((), ())),
            precision=lax.Precision.HIGHEST,
            preferred_element_type=F32,
        )
        total = part if total is None else total + part
    for k in range(KB):
        r.gr[:, k, :] = total[k * 16 : k * 16 + 8]
        r.ur[:, k, :] = total[k * 16 + 8 : k * 16 + 16]
    for j in range(KB):
        rows = r.left[j]
        r.gl[:, j, :] = rows[:MS, :MB]
        r.ul[:, j, :] = rows[:MS, MB:]
        r.dr[:, j, :] = r.dright[j][:MS]
        r.dl[:, j, :] = r.dleft[j // 2][(j % 2) * 8 : (j % 2 + 1) * 8]
    for copy in copies[:2]:
        copy.wait()


def local(tokens, gate_right, gate_left, upward_right, upward_left, down_right, down_left, cotangent):
    scale = float(tokens.shape[0] * lax.axis_size("dp")) ** (-0.5)
    given = {
        "x": tokens,
        "g": cotangent,
        "wgr": jnp.transpose(gate_right, (1, 2, 0)),
        "wur": jnp.transpose(upward_right, (1, 2, 0)),
        "wdl": down_left,
        "wgl": gate_left,
        "wul": upward_left,
        "wdr": down_right,
    }
    given.update({name: jnp.asarray(value) for name, value in permutations().items()})
    scratch = scratch_list()
    names = ["h_" + name for name in INPUTS] + list(OUTS) + [name for name, _ in scratch]
    shapes = [jax.ShapeDtypeStruct((T, KB * DB), BF)] * 2
    shapes += [jax.ShapeDtypeStruct((count, 16, lanes), F32) for _, count, lanes in GROUPS]

    def body(*refs):
        kernel(scale, names, *refs)

    results = pl.pallas_call(
        body,
        out_shape=shapes,
        in_specs=[pl.BlockSpec(memory_space=pl.ANY)] * len(INPUTS),
        out_specs=[pl.BlockSpec(memory_space=pltpu.VMEM)] * len(OUTS),
        scratch_shapes=[shape for _, shape in scratch],
        compiler_params=pltpu.CompilerParams(
            collective_id=0, has_side_effects=True, vmem_limit_bytes=VMEM_LIMIT
        ),
        name="monarch",
    )(*[given[name] for name in INPUTS])

    last = [
        ((T, KB * DB), BF),
        ((T, KB * DB), BF),
        ((8, KB, MB), F32),
        ((MS, KB, MB), F32),
        ((8, KB, MB), F32),
        ((MS, KB, MB), F32),
        ((MS, KB, DB), F32),
        ((8, KB, DB), F32),
    ]
    anywhere, vmem = pl.BlockSpec(memory_space=pl.ANY), pl.BlockSpec(memory_space=pltpu.VMEM)
    parts = list(results[2:]) + [jnp.asarray(untangle())]
    names = ["mixed_in", "gtok_in"] + ["h_" + name for name in UNPACKED]
    names += ["mixed", "gtok", "gr", "gl", "ur", "ul", "dr", "dl"] + list(UNPACKED) + ["sem"]
    return pl.pallas_call(
        lambda *refs: unpack(names, *refs),
        out_shape=[jax.ShapeDtypeStruct(*entry) for entry in last],
        in_specs=[anywhere] * (2 + len(parts)),
        out_specs=[vmem] * 8,
        scratch_shapes=[pltpu.VMEM(part.shape, F32) for part in parts]
        + [pltpu.SemaphoreType.DMA((2 + len(parts),))],
        compiler_params=pltpu.CompilerParams(vmem_limit_bytes=VMEM_LIMIT),
        name="unpack",
    )(*results[:2], *parts)


def solution(mesh):
    weight = P(None, "blk", None)
    grad = P("dp", "blk", None)
    return jax.shard_map(
        local,
        mesh=mesh,
        in_specs=(P("dp", "blk"),) + (weight,) * 6 + (P("dp", "blk"),),
        out_specs=(P("dp", "blk"),) * 2 + (grad,) * 6,
        check_vma=False,
    )
```

time: 118 us -> 94.3 us (0.80)
  local copies, waits for them, and re-layouts: 18.5 us -> 0 us
  Pallas kernels: 98.3 us -> 93.4 us
    pallas_call x1, Pallas kernels: 98.3 us -> 90.1 us  [local(): pl.pallas_call(body, out_shape=shapes, in_specs=[pl.BlockSpec(memory_spac...]
    unnamed x13 -> x0, local copies, waits for them, and re-layouts: 7.93 us -> none
    transpose x5 -> x0, local copies, waits for them, and re-layouts: 5.85 us -> none  [the longest x1 4.04 us: local(): jnp.transpose(upward_left, (1, 0, 2))]
    reshape x5 -> x0, local copies, waits for them, and re-layouts: 4.67 us -> none  [the longest x4 3.23 us: unpack(): return right.reshape(2, 8, 2, MB).transpose(1, 0, 2, 3).reshape(8, KB, MB)]
    pallas_call x0 -> x1, Pallas kernels: none -> 3.3 us  [local(): pl.pallas_call(lambda *refs: unpack(names, *refs), out_shape=[jax.ShapeDt...]
where the time goes in v2:
time: 94.3 us; the launch traced here: 94.2 us
  Pallas kernels  93.4 us (99%)
    pallas_call x1, Pallas kernels, local(): pl.pallas_call(body, out_shape=shapes, in_specs=[pl.BlockSpec(memory_spac...  90.1 us
    pallas_call x1, Pallas kernels, local(): pl.pallas_call(lambda *refs: unpack(names, *refs), out_shape=[jax.ShapeDt...  3.3 us

profile of v2, /device:TPU:1, one launch (start us, length us, event | category | flops | bytes accessed | tf_op | source)
XLA Modules:
  0.0 94.2 jit_solution(3274664242390523827)
XLA Ops:
  0.6 90.1 %monarch.1 = (bf16[128,1024]{1,0:T(8,128)(2,1)}, bf16[128,1024]{1,0:T(8,128)(2,1)}, f32[4,16,896]{2,1,0:T(8,128)}, f32[4,16,256]{2,1,0:T(8,128)}, f32[2,16,256]{...) custom-call(bf16[128,1024]{1,0:T(8,128)(2,1)} %refs_0_.1, bf16[4,448,256]{2,1,0:T(8,128)(2,1)} %bitcast.2, ...), custom_call_target="tpu_custom_call" | custom-call | tf_op jit(solution)/shard_map/monarch/pallas_call | solution.py:560
  90.8 3.3 %unpack.1 = (bf16[128,1024]{1,0:T(8,128)(2,1)}, bf16[128,1024]{1,0:T(8,128)(2,1)}, f32[8,4,448]{2,1,0:T(4,128)}, f32[14,4,448]{2,1,0:T(4,128)}, f32[8,4,448]{2,1...) custom-call(bf16[128,1024]{1,0:T(8,128)(2,1)} %get-tuple-element.15.refs_0_, ...), custom_call_target="tpu_custom_call" | custom-call | tf_op jit(solution)/shard_map/unpack/pallas_call | solution.py:586

commit v3 on v2

--- a/solution.py
+++ b/solution.py
@@ -102,6 +102,7 @@
     "spread",
     "twin",
 )
+FIRST = 4
 SHAPES = {
     "x": (T, KB * DB),
     "g": (T, KB * DB),
@@ -120,13 +121,16 @@
     "twin": (2, 512, 256),
 }
 GROUPS = (
-    ("left", 4, 896),
-    ("dright", 4, 256),
+    ("left0", 2, 896),
+    ("left1", 2, 896),
+    ("dright0", 2, 256),
+    ("dright1", 2, 256),
     ("dleft", 2, 256),
     ("right0", 1, 896),
     ("right1", 1, 896),
 )
-UNPACKED = ("left", "dright", "dleft", "right0", "right1", "columns")
+PAIRED = ("left0", "left1", "dright0", "dright1")
+UNPACKED = PAIRED + ("dleft", "right0", "right1", "columns")
 OUTS = ("mixed", "gtok") + tuple("o_" + name for name, _, _ in GROUPS)
 SLABS = (
     ("a0", (112, 256)),
@@ -183,8 +187,14 @@
         add("r0_" + name, (count, 256, lanes))
         add("s1_" + name, (count, X, 64, lanes))
         add("r1_" + name, (count, 3, 64, lanes))
-        add("s2_" + name, (count, Z, 16, lanes))
-        add("r2_" + name, (3, count, 16, lanes))
+        if name in PAIRED:
+            add("s2_" + name, (count, 2, 2, 16, lanes))
+            add("r2_" + name, (count, 2, 16, lanes))
+            add("s3_" + name, (count, 2, 16, lanes))
+            add("r3_" + name, (count, 16, lanes))
+        else:
+            add("s2_" + name, (count, Z, 16, lanes))
+            add("r2_" + name, (3, count, 16, lanes))
         for kind in ("ss0_", "rs0_"):
             out.append((kind + name, pltpu.SemaphoreType.DMA((count,))))
         for kind in ("ss1_", "rs1_"):
@@ -210,7 +220,12 @@
     loads = {}
     for i, name in enumerate(INPUTS):
         loads[name] = pltpu.make_async_copy(v["h_" + name], v["v_" + name], r.in_sem.at[i])
-        loads[name].start()
+
+    def load(*which):
+        for name in which:
+            loads[name].start()
+
+    load(*INPUTS[:FIRST])
 
     def need(*which):
         for name in which:
@@ -278,7 +293,8 @@
         gone = {id(copy) for copy in copies.values()}
         pending[:] = [copy for copy in pending if id(copy) not in gone]
 
-    need("x", "wgr", "wur", "take")
+    need(*INPUTS[:FIRST])
+    load(*INPUTS[FIRST:])
     for k in range(KB):
         xk = r.v_x[:, k * DB : (k + 1) * DB]
         r.flow[k, :, :T] = nt(r.v_wgr[k], xk)
@@ -389,6 +405,40 @@
                 s2.at[:, (z + i + 1) % Z], r2.at[i], ss.at[i], rs.at[i], z_ids[i]
             )
 
+    def start_pair(name, count):
+        s1, r1, s2, r2, ss, rs = (
+            v[k + name] for k in ("s1_", "r1_", "s2_", "r2_", "ss2_", "rs2_")
+        )
+        for j in range(count):
+            for i in range(3):
+                moves[name, 1, j, i].wait_recv()
+            total = s1[j, x].astype(F32)
+            for i in range(3):
+                total = total + r1[j, i].astype(F32)
+            s2[j] = total.astype(BF).reshape(s2.shape[1:])
+        near = z + 1 - 2 * (z % 2)
+        moves[name, 2] = remote(
+            s2.at[:, :, 1 - z % 2], r2, ss.at[0], rs.at[0], dp_id(near, x, core)
+        )
+
+    def start_far(name, count):
+        s2, r2, s3, r3, ss, rs = (
+            v[k + name] for k in ("s2_", "r2_", "s3_", "r3_", "ss2_", "rs2_")
+        )
+        moves[name, 2].wait_recv()
+        for j in range(count):
+            for i in range(2):
+                s3[j, i] = (s2[j, i, z % 2].astype(F32) + r2[j, i].astype(F32)).astype(BF)
+        moves[name, 3] = remote(
+            s3.at[:, 1 - z // 2], r3, ss.at[1], rs.at[1], dp_id((z + 2) % Z, x, core)
+        )
+
+    def finish_far(name, count):
+        s3, r3, out = v["s3_" + name], v["r3_" + name], v["o_" + name]
+        moves[name, 3].wait_recv()
+        for j in range(count):
+            out[j] = scale * (s3[j, z // 2].astype(F32) + r3[j].astype(F32))
+
     def finish(name, count):
         s2, r2, out = v["s2_" + name], v["r2_" + name], v["o_" + name]
         for i in range(3):
@@ -406,12 +456,6 @@
             f = nt(r.v_spread[...], r.hidden[j]).astype(BF)
             r.lhs_dright[j] = f.reshape(2, 256, T)
 
-    def left_half(j, c):
-        return nn(r.lhs_left[j, c], r.rhs_left[j])
-
-    def dright_half(j, c):
-        return nt(r.lhs_dright[j, c], r.dback[j])
-
     def dleft_half(q, c):
         rows = [r.v_g[:, (2 * q + i) * DB : (2 * q + i + 1) * DB] for i in range(2)]
         return nn(r.lhs_dleft[q, c], jnp.concatenate(rows, axis=0))
@@ -438,12 +482,15 @@
         start_core("right%d" % h, (0,), right_half)
 
     def left(h):
-        which = (2 * h, 2 * h + 1)
         sides(h)
-        start_core("left", which, left_half)
-        start_core("dright", which, dright_half)
-        start_x("left", which, left_half)
-        start_x("dright", which, dright_half)
+        parts = [
+            ("left%d" % h, (0, 1), lambda i, c: nn(r.lhs_left[2 * h + i, c], r.rhs_left[2 * h + i])),
+            ("dright%d" % h, (0, 1), lambda i, c: nt(r.lhs_dright[2 * h + i, c], r.dback[2 * h + i])),
+        ]
+        for part in parts:
+            start_core(*part)
+        for part in parts:
+            start_x(*part)
 
     sent(from_a[0])
     from_c = exchange("c")
@@ -466,13 +513,17 @@
     for k in range(KB):
         r.tok[:, k * DB : (k + 1) * DB] = token_part(0, k)
     start_x("right0", (0,), right_half)
-    sent(from_d[1])
     from_b = [exchange("b0"), exchange("b1")]
 
+    for name in ("left0", "dright0", "left1", "dright1"):
+        start_pair(name, 2)
+
     right(1)
+    start_far("left0", 2)
+    start_far("dright0", 2)
     start_x("right1", (0,), right_half)
-    start_z("left", 4)
-    start_z("dright", 4)
+    start_far("left1", 2)
+    start_far("dright1", 2)
     start_z("right0", 1)
 
     for copies in from_b:
@@ -482,17 +533,17 @@
         f = nn(r.v_twin[j % 2], r.dseen[j]).astype(BF)
         r.lhs_dleft[j // 2, :, :, (j % 2) * T : (j % 2 + 1) * T] = f.reshape(2, 256, T)
     start_core("dleft", (0, 1), dleft_half)
-    start_x("dleft", (0, 1), dleft_half)
     for k in range(KB):
         columns = slice(k * DB, (k + 1) * DB)
         r.gtok[:, columns] = (r.tok[:, columns] + token_part(1, k)).astype(BF)
+    start_x("dleft", (0, 1), dleft_half)
     start_z("right1", 1)
     for j in range(KB):
         r.mixed[:, j * DB : (j + 1) * DB] = tn(r.dseen[j], r.dl[j]).astype(BF)
     start_z("dleft", 2)
-    finish("left", 4)
-    finish("dright", 4)
     finish("right0", 1)
+    for name in PAIRED:
+        finish_far(name, 2)
     finish("right1", 1)
     finish("dleft", 2)
     for copy in pending:
@@ -527,10 +578,10 @@
         r.gr[:, k, :] = total[k * 16 : k * 16 + 8]
         r.ur[:, k, :] = total[k * 16 + 8 : k * 16 + 16]
     for j in range(KB):
-        rows = r.left[j]
+        rows = (r.left0, r.left1)[j // 2][j % 2]
         r.gl[:, j, :] = rows[:MS, :MB]
         r.ul[:, j, :] = rows[:MS, MB:]
-        r.dr[:, j, :] = r.dright[j][:MS]
+        r.dr[:, j, :] = (r.dright0, r.dright1)[j // 2][j % 2][:MS]
         r.dl[:, j, :] = r.dleft[j // 2][(j % 2) * 8 : (j % 2 + 1) * 8]
     for copy in copies[:2]:
         copy.wait()

time: 94.3 us -> 91.9 us (0.975)
  Pallas kernels: 93.4 us -> 90.9 us
    pallas_call x1, Pallas kernels: 90.1 us -> 87.6 us  [local(): pl.pallas_call(body, out_shape=shapes, in_specs=[pl.BlockSpec(memory_spac...]
where the time goes in v3:
time: 91.9 us; the launch traced here: 91.8 us
  Pallas kernels  90.9 us (99%)
    pallas_call x1, Pallas kernels, local(): pl.pallas_call(body, out_shape=shapes, in_specs=[pl.BlockSpec(memory_spac...  87.6 us
    pallas_call x1, Pallas kernels, local(): pl.pallas_call(lambda *refs: unpack(names, *refs), out_shape=[jax.ShapeDt...  3.33 us

profile of v3, /device:TPU:1, one launch (start us, length us, event | category | flops | bytes accessed | tf_op | source)
XLA Modules:
  0.0 91.8 jit_solution(15770412858417202110)
XLA Ops:
  0.6 87.6 %monarch.1 = (bf16[128,1024]{1,0:T(8,128)(2,1)}, bf16[128,1024]{1,0:T(8,128)(2,1)}, f32[2,16,896]{2,1,0:T(8,128)}, f32[2,16,896]{2,1,0:T(8,128)}, f32[2,16,256]{...) custom-call(bf16[128,1024]{1,0:T(8,128)(2,1)} %refs_0_.1, ...), custom_call_target="tpu_custom_call" | custom-call | tf_op jit(solution)/shard_map/monarch/pallas_call | solution.py:611
  88.2 3.3 %unpack.1 = (bf16[128,1024]{1,0:T(8,128)(2,1)}, bf16[128,1024]{1,0:T(8,128)(2,1)}, f32[8,4,448]{2,1,0:T(4,128)}, f32[14,4,448]{2,1,0:T(4,128)}, f32[8,4,448]{2,1...) custom-call(bf16[128,1024]{1,0:T(8,128)(2,1)} %get-tuple-element.17.refs_0_, ...), custom_call_target="tpu_custom_call" | custom-call | tf_op jit(solution)/shard_map/unpack/pallas_call | solution.py:637

commit v4 on v3

--- a/solution.py
+++ b/solution.py
@@ -182,6 +182,9 @@
     add("rhs_gright", (896, 512))
     add("rhs_uright", (896, 512))
     add("tok", (T, KB * DB), F32)
+    add("w_mixed", (T, KB * DB))
+    add("w_gtok", (T, KB * DB))
+    out.append(("out_sem", pltpu.SemaphoreType.DMA((2,))))
     for name, count, lanes in GROUPS:
         add("s0_" + name, (count, 256, lanes))
         add("r0_" + name, (count, 256, lanes))
@@ -535,17 +538,23 @@
     start_core("dleft", (0, 1), dleft_half)
     for k in range(KB):
         columns = slice(k * DB, (k + 1) * DB)
-        r.gtok[:, columns] = (r.tok[:, columns] + token_part(1, k)).astype(BF)
+        r.w_gtok[:, columns] = (r.tok[:, columns] + token_part(1, k)).astype(BF)
+    out_gtok = pltpu.make_async_copy(r.w_gtok, r.gtok, r.out_sem.at[0])
+    out_gtok.start()
     start_x("dleft", (0, 1), dleft_half)
     start_z("right1", 1)
     for j in range(KB):
-        r.mixed[:, j * DB : (j + 1) * DB] = tn(r.dseen[j], r.dl[j]).astype(BF)
+        r.w_mixed[:, j * DB : (j + 1) * DB] = tn(r.dseen[j], r.dl[j]).astype(BF)
+    out_mixed = pltpu.make_async_copy(r.w_mixed, r.mixed, r.out_sem.at[1])
+    out_mixed.start()
     start_z("dleft", 2)
     finish("right0", 1)
     for name in PAIRED:
         finish_far(name, 2)
     finish("right1", 1)
     finish("dleft", 2)
+    out_gtok.wait()
+    out_mixed.wait()
     for copy in pending:
         copy.wait_send()
 
@@ -553,15 +562,21 @@
 def unpack(names, *refs):
     r = types.SimpleNamespace(**dict(zip(names, refs)))
     copies = [
-        pltpu.make_async_copy(r.mixed_in, r.mixed, r.sem.at[0]),
-        pltpu.make_async_copy(r.gtok_in, r.gtok, r.sem.at[1]),
+        pltpu.make_async_copy(r.mixed_in, r.mixed_held, r.sem.at[0]),
+        pltpu.make_async_copy(r.gtok_in, r.gtok_held, r.sem.at[1]),
     ]
     for i, name in enumerate(UNPACKED):
         copies.append(pltpu.make_async_copy(vars(r)["h_" + name], vars(r)[name], r.sem.at[2 + i]))
     for copy in copies:
         copy.start()
-    for copy in copies[2:]:
+    for copy in copies:
         copy.wait()
+    onward = [
+        pltpu.make_async_copy(r.mixed_held, r.mixed, r.out_sem.at[0]),
+        pltpu.make_async_copy(r.gtok_held, r.gtok, r.out_sem.at[1]),
+    ]
+    for copy in onward:
+        copy.start()
     total = None
     for h, source in enumerate((r.right0, r.right1)):
         rows = source[0]
@@ -583,7 +598,7 @@
         r.ul[:, j, :] = rows[:MS, MB:]
         r.dr[:, j, :] = (r.dright0, r.dright1)[j // 2][j % 2][:MS]
         r.dl[:, j, :] = r.dleft[j // 2][(j % 2) * 8 : (j % 2 + 1) * 8]
-    for copy in copies[:2]:
+    for copy in onward:
         copy.wait()
 
 
@@ -612,7 +627,8 @@
         body,
         out_shape=shapes,
         in_specs=[pl.BlockSpec(memory_space=pl.ANY)] * len(INPUTS),
-        out_specs=[pl.BlockSpec(memory_space=pltpu.VMEM)] * len(OUTS),
+        out_specs=[pl.BlockSpec(memory_space=pl.ANY)] * 2
+        + [pl.BlockSpec(memory_space=pltpu.VMEM)] * (len(OUTS) - 2),
         scratch_shapes=[shape for _, shape in scratch],
         compiler_params=pltpu.CompilerParams(
             collective_id=0, has_side_effects=True, vmem_limit_bytes=VMEM_LIMIT
@@ -633,14 +649,16 @@
     anywhere, vmem = pl.BlockSpec(memory_space=pl.ANY), pl.BlockSpec(memory_space=pltpu.VMEM)
     parts = list(results[2:]) + [jnp.asarray(untangle())]
     names = ["mixed_in", "gtok_in"] + ["h_" + name for name in UNPACKED]
-    names += ["mixed", "gtok", "gr", "gl", "ur", "ul", "dr", "dl"] + list(UNPACKED) + ["sem"]
+    names += ["mixed", "gtok", "gr", "gl", "ur", "ul", "dr", "dl"] + list(UNPACKED)
+    names += ["mixed_held", "gtok_held", "sem", "out_sem"]
     return pl.pallas_call(
         lambda *refs: unpack(names, *refs),
         out_shape=[jax.ShapeDtypeStruct(*entry) for entry in last],
         in_specs=[anywhere] * (2 + len(parts)),
-        out_specs=[vmem] * 8,
+        out_specs=[anywhere] * 2 + [vmem] * 6,
         scratch_shapes=[pltpu.VMEM(part.shape, F32) for part in parts]
-        + [pltpu.SemaphoreType.DMA((2 + len(parts),))],
+        + [pltpu.VMEM((T, KB * DB), BF)] * 2
+        + [pltpu.SemaphoreType.DMA((2 + len(parts),)), pltpu.SemaphoreType.DMA((2,))],
         compiler_params=pltpu.CompilerParams(vmem_limit_bytes=VMEM_LIMIT),
         name="unpack",
     )(*results[:2], *parts)

time: 91.9 us -> 91.5 us (level)
  no operation moved by 1% of the time
where the time goes in v4:
time: 91.5 us; the launch traced here: 91.3 us
  Pallas kernels  90.5 us (99%)
    pallas_call x1, Pallas kernels, local(): pl.pallas_call(body, out_shape=shapes, in_specs=[pl.BlockSpec(memory_spac...  87.3 us
    pallas_call x1, Pallas kernels, local(): pl.pallas_call(lambda *refs: unpack(names, *refs), out_shape=[jax.ShapeDt...  3.2 us

profile of v4, /device:TPU:1, one launch (start us, length us, event | category | flops | bytes accessed | tf_op | source)
XLA Modules:
  0.0 91.3 jit_solution(1318885529225436567)
XLA Ops:
  0.6 87.3 %monarch.1 = (bf16[128,1024]{1,0:T(8,128)(2,1)}, bf16[128,1024]{1,0:T(8,128)(2,1)}, f32[2,16,896]{2,1,0:T(8,128)}, f32[2,16,896]{2,1,0:T(8,128)}, f32[2,16,256]{...) custom-call(bf16[128,1024]{1,0:T(8,128)(2,1)} %refs_0_.1, ...), custom_call_target="tpu_custom_call" | custom-call | tf_op jit(solution)/shard_map/monarch/pallas_call | solution.py:626
  88.0 3.2 %unpack.1 = (bf16[128,1024]{1,0:T(8,128)(2,1)}, bf16[128,1024]{1,0:T(8,128)(2,1)}, f32[8,4,448]{2,1,0:T(4,128)}, f32[14,4,448]{2,1,0:T(4,128)}, f32[8,4,448]{2,1...) custom-call(bf16[128,1024]{1,0:T(8,128)(2,1)} %get-tuple-element.17.refs_0_, ...), custom_call_target="tpu_custom_call" | custom-call | tf_op jit(solution)/shard_map/unpack/pallas_call | solution.py:654

commit v5 on v4

--- a/solution.py
+++ b/solution.py
@@ -543,11 +543,11 @@
     out_gtok.start()
     start_x("dleft", (0, 1), dleft_half)
     start_z("right1", 1)
+    start_z("dleft", 2)
     for j in range(KB):
         r.w_mixed[:, j * DB : (j + 1) * DB] = tn(r.dseen[j], r.dl[j]).astype(BF)
     out_mixed = pltpu.make_async_copy(r.w_mixed, r.mixed, r.out_sem.at[1])
     out_mixed.start()
-    start_z("dleft", 2)
     finish("right0", 1)
     for name in PAIRED:
         finish_far(name, 2)

time: 91.5 us -> 91.5 us (level)
  no operation moved by 1% of the time
where the time goes in v5:
time: 91.5 us; the launch traced here: 91.3 us
  Pallas kernels  90.5 us (99%)
    pallas_call x1, Pallas kernels, local(): pl.pallas_call(body, out_shape=shapes, in_specs=[pl.BlockSpec(memory_spac...  87.3 us
    pallas_call x1, Pallas kernels, local(): pl.pallas_call(lambda *refs: unpack(names, *refs), out_shape=[jax.ShapeDt...  3.2 us

profile of v5, /device:TPU:1, one launch (start us, length us, event | category | flops | bytes accessed | tf_op | source)
XLA Modules:
  0.0 91.3 jit_solution(7109133600796994036)
XLA Ops:
  0.6 87.3 %monarch.1 = (bf16[128,1024]{1,0:T(8,128)(2,1)}, bf16[128,1024]{1,0:T(8,128)(2,1)}, f32[2,16,896]{2,1,0:T(8,128)}, f32[2,16,896]{2,1,0:T(8,128)}, f32[2,16,256]{...) custom-call(bf16[128,1024]{1,0:T(8,128)(2,1)} %refs_0_.1, ...), custom_call_target="tpu_custom_call" | custom-call | tf_op jit(solution)/shard_map/monarch/pallas_call | solution.py:626
  88.0 3.2 %unpack.1 = (bf16[128,1024]{1,0:T(8,128)(2,1)}, bf16[128,1024]{1,0:T(8,128)(2,1)}, f32[8,4,448]{2,1,0:T(4,128)}, f32[14,4,448]{2,1,0:T(4,128)}, f32[8,4,448]{2,1...) custom-call(bf16[128,1024]{1,0:T(8,128)(2,1)} %get-tuple-element.17.refs_0_, ...), custom_call_target="tpu_custom_call" | custom-call | tf_op jit(solution)/shard_map/unpack/pallas_call | solution.py:654
